TPU v7x, 32 devices: a whole 2x2x4 slice. The times are simulated.
32 devices in a mesh: parts: 2 (over y), ep: 4 (over z), dp: 2 (over x), tp: 2 (over core).
Axes of the slice: x: 2, y: 2, z: 4, core: 2. Of those that a mesh axis runs over, the one named last changes fastest.
Arguments:
- latent_in: bfloat16 [2048, 1024], P(('parts', 'ep', 'dp')), parts along dimension 0, may hold values from -6 to 6
- out_grad: bfloat16 [2048, 1024], P(('parts', 'ep', 'dp')), parts along dimension 0, may hold values from -6 to 6
- expert_ids: int32 [2048, 2], P(('parts', 'ep', 'dp')), parts along dimension 0, may hold values from 0 to 3, all different within a row; in each aligned block of 128 rows (0 to 127, 128 to 255, ...) at most 72 rows name the same one
- gate_weights: bfloat16 [2048, 2], P(('parts', 'ep', 'dp')), parts along dimension 0, may hold values from 0.049804688 to 0.5
- up_weight: bfloat16 [4, 1024, 1024], P('ep', None, 'tp'), may hold values from -0.1875 to 0.1875
- down_weight: bfloat16 [4, 1024, 1024], P('ep', 'tp'), may hold values from -0.1875 to 0.1875
Outputs:
- latent_out: bfloat16 [2048, 1024], P(('parts', 'ep', 'dp'), 'tp'), parts along dimension 0
- latent_grad: bfloat16 [2048, 1024], P(('parts', 'ep', 'dp'), 'tp'), parts along dimension 0
- grad_up: float32 [8, 1024, 1024], P(('parts', 'ep'), 'dp', 'tp'), parts along dimension 0
- grad_down: float32 [8, 1024, 1024], P(('parts', 'ep'), 'tp', 'dp'), parts along dimension 0
There are 2 independent parts, one for each index of `parts`. A program takes and returns all parts, laid end to end along the dimension named above; an argument that names none is the same for every part. Nothing has to cross between parts.
Inputs may be any that keep to these rules, and one draw needn't show every extreme that they name: `expert_ids`: each row names 2 different experts. In the 128 rows of one device no expert is named more than 72 times, a bound that some block reaches.
All inputs are finite; a program needn't handle non-finite values.
Results may differ from a plain program's by a relative error of at most 0.011.
Values may be sent and summed in bfloat16 or wider, within the bound.
A program may use at most 64 MiB of HBM per device.

v0:
```python
import jax
import jax.numpy as jnp
from jax import lax
from jax.sharding import PartitionSpec as P


def to_blocks(latent_cols, grad_cols, source, weight_matrix, experts_all, capacity):
    zero_row = jnp.zeros((1, latent_cols.shape[1]), jnp.bfloat16)
    gathered = jnp.concatenate([latent_cols, zero_row], axis=0)[source]
    padded_grad = jnp.concatenate([grad_cols, zero_row], axis=0)[source]
    scaled = (weight_matrix.astype(jnp.float32)[:, None] * padded_grad.astype(jnp.float32)).astype(
        jnp.bfloat16
    )
    return (
        gathered.reshape(experts_all, capacity, latent_cols.shape[1]),
        scaled.reshape(experts_all, capacity, latent_cols.shape[1]),
    )


def body(latent_in, out_grad, expert_ids, gate_weights, up_weight, down_weight):
    tok_rows, latent_width = latent_in.shape
    fanout = expert_ids.shape[1]
    exp_local = up_weight.shape[0]
    ep_count = lax.axis_size("ep")
    experts_all = exp_local * ep_count
    capacity = 9 * tok_rows * fanout // (8 * experts_all)
    slot_count = experts_all * capacity
    flat_ids = expert_ids.reshape(-1)
    onehot = (flat_ids[:, None] == jnp.arange(experts_all, dtype=jnp.int32)[None, :]).astype(
        jnp.int32
    )
    position = jnp.sum(jnp.cumsum(onehot, axis=0) * onehot, axis=1) - 1
    target = flat_ids * capacity + position
    owning = jnp.arange(tok_rows * fanout, dtype=jnp.int32) // fanout
    source = jnp.full((slot_count,), tok_rows, jnp.int32).at[target].set(owning)
    weight_matrix = jnp.zeros((slot_count,), jnp.bfloat16).at[target].set(gate_weights.reshape(-1))
    rows_in, grads_in = to_blocks(latent_in, out_grad, source, weight_matrix, experts_all, capacity)
    recv_rows, recv_grads = (
        lax.all_to_all(rows_in, "ep", split_axis=0, concat_axis=1, tiled=True),
        lax.all_to_all(grads_in, "ep", split_axis=0, concat_axis=1, tiled=True),
    )
    preact = jnp.einsum("erl,elf->erf", recv_rows, up_weight, preferred_element_type=jnp.float32)
    positive = jnp.maximum(preact, 0.0)
    hidden_state = (positive * positive).astype(jnp.bfloat16)
    output_part = jnp.einsum(
        "erf,efl->erl", hidden_state, down_weight, preferred_element_type=jnp.float32
    ).astype(jnp.bfloat16)
    hidden_grad = jnp.einsum(
        "erl,efl->erf", recv_grads, down_weight, preferred_element_type=jnp.float32
    )
    preact_grad = (2.0 * hidden_grad * positive).astype(jnp.bfloat16)
    input_part = jnp.einsum(
        "erf,elf->erl", preact_grad, up_weight, preferred_element_type=jnp.float32
    ).astype(jnp.bfloat16)
    up_partial = jnp.einsum(
        "erl,erf->elf", recv_rows, preact_grad, preferred_element_type=jnp.float32
    )
    down_partial = jnp.einsum(
        "erf,erl->efl", hidden_state, recv_grads, preferred_element_type=jnp.float32
    )
    grad_up, grad_down = (
        lax.psum_scatter(
            up_partial.astype(jnp.bfloat16), "dp", scatter_dimension=1, tiled=True
        ).astype(jnp.float32),
        lax.psum_scatter(
            down_partial.astype(jnp.bfloat16), "dp", scatter_dimension=2, tiled=True
        ).astype(jnp.float32),
    )
    back_out, back_in = (
        lax.all_to_all(output_part, "ep", split_axis=1, concat_axis=0, tiled=True),
        lax.all_to_all(input_part, "ep", split_axis=1, concat_axis=0, tiled=True),
    )
    picked_out = back_out.reshape(slot_count, latent_width)[target].reshape(
        tok_rows, fanout, latent_width
    )
    picked_in = back_in.reshape(slot_count, latent_width)[target].reshape(
        tok_rows, fanout, latent_width
    )
    token_out = jnp.einsum(
        "tk,tkl->tl", gate_weights, picked_out, preferred_element_type=jnp.float32
    )
    token_in = jnp.sum(picked_in.astype(jnp.float32), axis=1)
    output_portion, in_share = (
        lax.psum_scatter(
            token_out.astype(jnp.bfloat16), "tp", scatter_dimension=1, tiled=True
        ).astype(jnp.float32),
        lax.psum_scatter(
            token_in.astype(jnp.bfloat16), "tp", scatter_dimension=1, tiled=True
        ).astype(jnp.float32),
    )
    return (output_portion.astype(jnp.bfloat16), in_share.astype(jnp.bfloat16), grad_up, grad_down)


def solution(mesh):
    return jax.shard_map(
        body,
        mesh=mesh,
        in_specs=(
            P(("parts", "ep", "dp"), None),
            P(("parts", "ep", "dp"), None),
            P(("parts", "ep", "dp"), None),
            P(("parts", "ep", "dp"), None),
            P("ep", None, "tp"),
            P("ep", "tp", None),
        ),
        out_specs=(
            P(("parts", "ep", "dp"), "tp"),
            P(("parts", "ep", "dp"), "tp"),
            P(("parts", "ep"), "dp", "tp"),
            P(("parts", "ep"), "tp", "dp"),
        ),
        check_vma=False,
    )
```

profile of v0, /device:TPU:9, one launch (start us, length us, event | category | flops | bytes accessed | tf_op | source)
XLA Modules:
  0.0 131.0 jit_solution(4608315628127988511)
XLA Ops:
  9.3 1.2 reduce-window.6
  11.0 1.4 %scatter_custom_fusion = s32[288]{0:T(512)S(1)} fusion(s32[256]{0:T(256)S(1)} %bitcast.78, s32[256]{0:T(256)S(1)} %and_select_fusion, s32[]{:T(128)} %constant.17.clone.1), kind=kCustom, calls=%fused_computation.42 | custom fusion | bytes 1156 | tf_op jit(solution)/shard_map/scatter | solution.py:35
  12.4 1.0 concatenate.6
  13.4 2.6 %gather_fusion = bf16[288,1024]{1,0:T(8,128)(2,1)} fusion(bf16[129,1024]{1,0:T(8,128)(2,1)S(1)} %concatenate.6, s32[1024]{0:T(1024)S(1)} %pad_clamp_fusion.1), kind=kCustom, calls=%fused_computation | custom fusion | bytes 1180800 | tf_op jit(solution)/shard_map/gather | solution.py:9
  16.0 4.9 %all-to-all-start = ((bf16[4,72,1024]{2,1,0:T(8,128)(2,1)}), bf16[4,72,1024]{2,1,0:T(8,128)(2,1)S(1)}, u32[]{:S(2)}, u32[]{:S(2)}) async-start(bf16[4,72,1024]{2,1,0:T(8,128)(2,1)} %bitcast.4), calls=%async_computation | async-start | bytes 1179648 | tf_op jit(solution)/shard_map/all_to_all | solution.py:39
  20.9 2.1 %gather_fusion.2 = bf16[288,1024]{1,0:T(8,128)(2,1)S(1)} fusion(bf16[129,1024]{1,0:T(8,128)(2,1)S(1)} %concatenate.7, s32[1024]{0:T(1024)S(1)} %pad_clamp_fusion.1), kind=kCustom, calls=%fused_computation.2 | custom fusion | bytes 1180800 | tf_op jit(solution)/shard_map/gather | solution.py:10
  23.3 2.2 %scatter_custom_fusion.1 = bf16[288]{0:T(512)(128)(2,1)S(1)} fusion(s32[256]{0:T(256)S(1)} %bitcast.79, bf16[256]{0:T(256)(128)(2,1)S(1)} %reshape.203, bf16[]{:T(256)} %constant.16.clone.1), kind=kCustom, calls=%fused_computation.44 | custom fusion | bytes 578 | tf_op jit(solution)/shard_map/scatter | solution.py:36
  25.5 1.0 fusion.6
  26.5 6.3 %all-to-all-done = bf16[4,72,1024]{2,1,0:T(8,128)(2,1)S(1)} async-done(((bf16[4,72,1024]{2,1,0:T(8,128)(2,1)}), bf16[4,72,1024]{2,1,0:T(8,128)(2,1)S(1)}, u32[]{:S(2)}, u32[]{:S(2)}) %all-to-all-start) | async-done | bytes 589856 | tf_op jit(solution)/shard_map/all_to_all | solution.py:39
  32.9 0.8 copy-done.2
  33.7 6.9 %all-to-all-start.2 = ((bf16[4,72,1024]{2,1,0:T(8,128)(2,1)}), bf16[4,72,1024]{2,1,0:T(8,128)(2,1)S(1)}, u32[]{:S(2)}, u32[]{:S(2)}) async-start(bf16[4,72,1024]{2,1,0:T(8,128)(2,1)} %fusion.6), calls=%async_computation.3 | async-start | bytes 1179648 | tf_op jit(solution)/shard_map/all_to_all | solution.py:40
  40.5 1.5 %convolution_maximum_fusion = f32[288,512]{1,0:T(8,128)S(1)} fusion(bf16[288,1024]{1,0:T(8,128)(2,1)} %bitcast.75, bf16[1,1024,512]{2,1,0:T(8,128)(2,1)S(1)} %copy-done.1), kind=kOutput, calls=%fused_computation.16 | convolution fusion | flops 302137344 | bytes 2228224 | tf_op jit(solution)/shard_map/erl,elf->erf/dot_general | solution.py:42
  42.1 10.3 %all-to-all-done.2 = bf16[4,72,1024]{2,1,0:T(8,128)(2,1)S(1)} async-done(((bf16[4,72,1024]{2,1,0:T(8,128)(2,1)}), bf16[4,72,1024]{2,1,0:T(8,128)(2,1)S(1)}, u32[]{:S(2)}, u32[]{:S(2)}) %all-to-all-start.2) | async-done | bytes 589856 | tf_op jit(solution)/shard_map/all_to_all | solution.py:40
  53.6 1.7 %fusion = bf16[1,1024,512]{2,1,0:T(8,128)(2,1)} fusion(bf16[288,1024]{1,0:T(8,128)(2,1)S(1)} %bitcast.76, bf16[288,512]{1,0:T(8,128)(2,1)S(1)} %fusion.5), kind=kOutput, calls=%fused_computation.8 | convolution fusion | flops 302514176 | bytes 1933312 | tf_op jit(solution)/shard_map/erl,erf->elf/dot_general | solution.py:55
  55.6 1.7 %fusion.1 = bf16[1,512,1024]{2,1,0:T(8,128)(2,1)} fusion(bf16[288,1024]{1,0:T(8,128)(2,1)S(1)} %bitcast.69, f32[288,512]{1,0:T(8,128)S(1)} %convolution_maximum_fusion), kind=kOutput, calls=%fused_computation.9 | convolution fusion | flops 302809088 | bytes 2228224 | tf_op jit(solution)/shard_map/erf,erl->efl/dot_general | solution.py:58
  57.8 0.9 copy.49
  59.2 4.9 %reduce.1 = bf16[288,1024]{1,0:T(8,128)(2,1)} reduce(bf16[288,1,1024]{2,1,0:T(2,128)(2,1)S(1)} %bitcast.70, bf16[]{:T(256)} %broadcast.107), dimensions={1}, to_apply=%bitcast.65.reduce_sub_computation | reduce | bytes 1179650
  64.1 2.3 %reshape.215 = bf16[4,2,36864]{2,1,0:T(2,128)(2,1)} reshape(bf16[288,1024]{1,0:T(8,128)(2,1)} %reduce.1) | data formatting | bytes 1179648
  66.5 7.7 %all-to-all-start.1 = ((bf16[4,2,36864]{2,1,0:T(2,128)(2,1)}), bf16[4,2,36864]{2,1,0:T(2,128)(2,1)}, u32[]{:S(2)}, u32[]{:S(2)}) async-start(bf16[4,2,36864]{2,1,0:T(2,128)(2,1)} %reshape.215), calls=%async_computation.1 | async-start | bytes 1179648 | tf_op jit(solution)/shard_map/all_to_all | solution.py:70
  74.8 0.9 copy.48
  75.7 4.1 %reduce.2 = bf16[288,1024]{1,0:T(8,128)(2,1)S(1)} reduce(bf16[288,1,1024]{2,1,0:T(2,128)(2,1)S(1)} %bitcast.71, bf16[]{:T(256)} %broadcast.107), dimensions={1}, to_apply=%bitcast.64.reduce_sub_computation | reduce | bytes 1179650
  79.8 1.2 reshape.217
  81.0 5.0 %all-to-all-done.1 = bf16[4,2,36864]{2,1,0:T(2,128)(2,1)} async-done(((bf16[4,2,36864]{2,1,0:T(2,128)(2,1)}), bf16[4,2,36864]{2,1,0:T(2,128)(2,1)}, u32[]{:S(2)}, u32[]{:S(2)}) %all-to-all-start.1) | async-done | bytes 589856 | tf_op jit(solution)/shard_map/all_to_all | solution.py:70
  85.9 7.1 %all-to-all-start.3 = ((bf16[4,2,36864]{2,1,0:T(2,128)(2,1)}), bf16[4,2,36864]{2,1,0:T(2,128)(2,1)S(1)}, u32[]{:S(2)}, u32[]{:S(2)}) async-start(bf16[4,2,36864]{2,1,0:T(2,128)(2,1)} %reshape.217), calls=%async_computation.4 | async-start | bytes 1179648 | tf_op jit(solution)/shard_map/all_to_all | solution.py:71
  93.1 2.3 %reshape.216 = bf16[288,1,1024]{2,1,0:T(2,128)(2,1)S(1)} reshape(bf16[4,2,36864]{2,1,0:T(2,128)(2,1)} %all-to-all-done.1) | data formatting | bytes 1179648
  95.5 1.2 gather_fusion.1
  98.5 6.4 %all-to-all-done.3 = bf16[4,2,36864]{2,1,0:T(2,128)(2,1)S(1)} async-done(((bf16[4,2,36864]{2,1,0:T(2,128)(2,1)}), bf16[4,2,36864]{2,1,0:T(2,128)(2,1)S(1)}, u32[]{:S(2)}, u32[]{:S(2)}) %all-to-all-start.3) | async-done | bytes 589856 | tf_op jit(solution)/shard_map/all_to_all | solution.py:71
  105.7 1.2 gather_fusion.3
  107.0 2.1 %reduce_sum.22 = bf16[128,1024]{1,0:T(8,128)(2,1)} reduce(bf16[128,2,1024]{2,1,0:T(2,128)(2,1)S(1)} %reshape.156, bf16[]{:T(256)} %constant.16.clone.1), dimensions={1}, to_apply=%region_6.7 | reduce | flops 131072 | bytes 786434 | tf_op jit(solution)/shard_map/reduce_sum | solution.py:82
  109.2 2.1 %convert_element_type.77 = f32[1,512,512]{2,1,0:T(8,128)} convert(bf16[1,512,512]{2,1,0:T(8,128)(2,1)} %reduce-scatter.9.cloned.1.call-done) | non-fusion elementwise | flops 262144 | bytes 1572864 | tf_op jit(solution)/shard_map/convert_element_type | solution.py:64
  111.3 2.1 %convert_element_type.80 = f32[1,512,512]{2,1,0:T(8,128)} convert(bf16[1,512,512]{2,1,0:T(8,128)(2,1)} %reduce-scatter.11.cloned.1.call-done) | non-fusion elementwise | flops 262144 | bytes 1572864 | tf_op jit(solution)/shard_map/convert_element_type | solution.py:67
  113.5 11.0 %reduce-scatter.7.cloned.1.call-done = bf16[128,512]{1,0:T(8,128)(2,1)} async-done(((bf16[128,1024]{1,0:T(8,128)(2,1)}), bf16[128,512]{1,0:T(8,128)(2,1)}) %reduce-scatter.7.cloned.1.call-update) | async-done | bytes 131088 | tf_op jit(solution)/shard_map/reduce_scatter | solution.py:87
  (62 shorter events, 9.0 us)
Async XLA Ops:
  7.2 45.2 %copy-start = (bf16[1,512,1024]{2,1,0:T(8,128)(2,1)S(1)}, bf16[1,512,1024]{2,1,0:T(8,128)(2,1)}, u32[]{:S(2)}) copy-start(bf16[1,512,1024]{2,1,0:T(8,128)(2,1)} %param.11) | copy-start | bytes 3145732
  16.0 4.9 %copy-start.6 = (bf16[128,1024]{1,0:T(8,128)(2,1)S(1)}, bf16[128,1024]{1,0:T(8,128)(2,1)}, u32[]{:S(2)}) copy-start(bf16[128,1024]{1,0:T(8,128)(2,1)} %param.7) | copy-start | bytes 786436
  16.0 16.9 %all-to-all-start = ((bf16[4,72,1024]{2,1,0:T(8,128)(2,1)}), bf16[4,72,1024]{2,1,0:T(8,128)(2,1)S(1)}, u32[]{:S(2)}, u32[]{:S(2)}) async-start(bf16[4,72,1024]{2,1,0:T(8,128)(2,1)} %bitcast.4), calls=%async_computation | async-start | bytes 1179648 | tf_op jit(solution)/shard_map/all_to_all | solution.py:39
  20.9 2.1 %copy-start.7 = (bf16[128,2]{0,1:T(2,128)(2,1)S(1)}, bf16[128,2]{0,1:T(2,128)(2,1)}, u32[]{:S(2)}) copy-start(bf16[128,2]{0,1:T(2,128)(2,1)} %param.9) | copy-start | bytes 1540
  25.5 15.0 %copy-start.1 = (bf16[1,1024,512]{2,1,0:T(8,128)(2,1)S(1)}, bf16[1,1024,512]{2,1,0:T(8,128)(2,1)}, u32[]{:S(2)}) copy-start(bf16[1,1024,512]{2,1,0:T(8,128)(2,1)} %param.10) | copy-start | bytes 3145732
  32.9 0.8 copy-start.2
  33.7 18.7 %all-to-all-start.2 = ((bf16[4,72,1024]{2,1,0:T(8,128)(2,1)}), bf16[4,72,1024]{2,1,0:T(8,128)(2,1)S(1)}, u32[]{:S(2)}, u32[]{:S(2)}) async-start(bf16[4,72,1024]{2,1,0:T(8,128)(2,1)} %fusion.6), calls=%async_computation.3 | async-start | bytes 1179648 | tf_op jit(solution)/shard_map/all_to_all | solution.py:40
  40.5 68.7 %reduce-scatter.9.cloned.1.call-start = ((), (), s32[]{:S(2)}) async-start(), calls=%async_computation.10 | async-start | bytes 1572864 | tf_op jit(solution)/shard_map/reduce_scatter | solution.py:62
  52.4 1.2 copy-start.3
  52.9 0.7 copy-start.4
  55.3 56.0 %reduce-scatter.11.cloned.1.call-start = ((), (), s32[]{:S(2)}) async-start(), calls=%async_computation.11 | async-start | bytes 1572864 | tf_op jit(solution)/shard_map/reduce_scatter | solution.py:65
  64.1 10.1 %copy-start.5 = (bf16[288,512]{1,0:T(8,128)(2,1)S(1)}, bf16[288,512]{1,0:T(8,128)(2,1)}, u32[]{:S(2)}) copy-start(bf16[288,512]{1,0:T(8,128)(2,1)} %copy-done.4) | copy-start | bytes 884740
  66.5 19.5 %all-to-all-start.1 = ((bf16[4,2,36864]{2,1,0:T(2,128)(2,1)}), bf16[4,2,36864]{2,1,0:T(2,128)(2,1)}, u32[]{:S(2)}, u32[]{:S(2)}) async-start(bf16[4,2,36864]{2,1,0:T(2,128)(2,1)} %reshape.215), calls=%async_computation.1 | async-start | bytes 1179648 | tf_op jit(solution)/shard_map/all_to_all | solution.py:70
  85.9 18.9 %all-to-all-start.3 = ((bf16[4,2,36864]{2,1,0:T(2,128)(2,1)}), bf16[4,2,36864]{2,1,0:T(2,128)(2,1)S(1)}, u32[]{:S(2)}, u32[]{:S(2)}) async-start(bf16[4,2,36864]{2,1,0:T(2,128)(2,1)} %reshape.217), calls=%async_computation.4 | async-start | bytes 1179648 | tf_op jit(solution)/shard_map/all_to_all | solution.py:71
  93.0 20.4 %reduce-scatter.5.cloned.1.call-start = ((), (), s32[]{:S(2)}) async-start(), calls=%async_computation.8 | async-start | bytes 393216 | tf_op jit(solution)/shard_map/reduce_scatter | solution.py:84
  98.4 26.1 %reduce-scatter.7.cloned.1.call-start = ((), (), s32[]{:S(2)}) async-start(), calls=%async_computation.9 | async-start | bytes 393216 | tf_op jit(solution)/shard_map/reduce_scatter | solution.py:87
Sparse Core Ops, SparseCore 0:
  55.5 23.4 reduce-scatter.8
  81.3 20.3 reduce-scatter.10
  104.5 8.3 reduce-scatter.4
  115.6 8.8 reduce-scatter.6
where the time goes:
time: 132 us; the launch traced here: 131 us
  waiting for transfers between devices  39.1 us (30%)
  starting transfers between devices  26.8 us (20%)
  local copies, waits for them, and re-layouts  25.5 us (19%)
  other arithmetic  18.5 us (14%)
  between operations  14 us (11%)
  matrix products  7.14 us (5%)
    reduce_scatter x1, waiting for transfers between devices, body(): lax.psum_scatter(token_in.astype(jnp.bfloat16), 'tp', scatter_dimension=1...  11 us
    all_to_all x1, waiting for transfers between devices, body(): lax.all_to_all(grads_in, 'ep', split_axis=0, concat_axis=1, tiled=True)  10.3 us
    unnamed x26, local copies, waits for them, and re-layouts  9.85 us
    unnamed x3, other arithmetic  9.05 us
    all_to_all x1, starting transfers between devices, body(): lax.all_to_all(output_part, 'ep', split_axis=1, concat_axis=0, tiled=True)  7.65 us
    all_to_all x1, starting transfers between devices, body(): lax.all_to_all(input_part, 'ep', split_axis=1, concat_axis=0, tiled=True)  7.1 us
    all_to_all x1, starting transfers between devices, body(): lax.all_to_all(grads_in, 'ep', split_axis=0, concat_axis=1, tiled=True)  6.86 us
    all_to_all x1, waiting for transfers between devices, body(): lax.all_to_all(input_part, 'ep', split_axis=1, concat_axis=0, tiled=True)  6.4 us
  transfers between devices with their start and end apart: 8, of which 5 were waited for; matrix products, arithmetic and copies ran while one was open for 29% of the time, Pallas kernels for 0%

commit v1 on v0

v1 whole, which is shorter than its diff:
```python
import functools

import jax
import jax.numpy as jnp
from jax import lax
from jax.experimental import pallas as pl
from jax.experimental.pallas import tpu as pltpu
from jax.sharding import PartitionSpec as P

MESH = pl.DeviceIdType.MESH
NT = (((1,), (1,)), ((), ()))
TN = (((0,), (0,)), ((), ()))


def dot(a, b, dims=(((1,), (0,)), ((), ()))):
    return lax.dot_general(a, b, dims, preferred_element_type=jnp.float32)


def kernel(
    n_ep, n_dp, cap,
    x_ref, g_ref, ids_ref, gate_ref, up_hbm, down_hbm,
    out_ref, in_ref, gu_ref, gd_ref,
    up, down, disp, other, recv, b_up, b_dn, part, got, mine, ret, back, gu, gd, route,
    w_sem, z_send, z_recv, s_send, s_recv, x_send, x_recv, p_send, p_recv, r_send, r_recv, o_sem,
):
    z, d, c = lax.axis_index("ep"), lax.axis_index("dp"), lax.axis_index("tp")
    sib = 1 - c
    rows = 2 * cap
    tok, width = x_ref.shape
    half = width // 2
    fanout = ids_ref.shape[1]
    bf = jnp.bfloat16

    def peer(i):
        if n_ep == 4 and isinstance(i, int):
            return (z, z + 1 - 2 * lax.rem(z, 2), lax.rem(z + 2, 4), 3 - z)[i]
        return lax.rem(z + i, n_ep)

    def each(order, body):
        if n_ep == 4:
            for i in order:
                body(i)
        else:
            lax.fori_loop(1, n_ep, lambda i, _: (body(i), 0)[1], 0)

    barrier = pltpu.get_barrier_semaphore()

    def greet(i, _):
        pl.semaphore_signal(
            barrier, inc=1, device_id={"ep": lax.rem(z + i, n_ep)}, device_id_type=MESH)
        return 0

    lax.fori_loop(1, n_ep, greet, 0)
    for j in range(1, n_dp):
        pl.semaphore_signal(
            barrier, inc=1, device_id={"dp": lax.rem(d + j, n_dp)}, device_id_type=MESH)
    pl.semaphore_signal(barrier, inc=1, device_id={"tp": sib}, device_id_type=MESH)

    load_up = pltpu.make_async_copy(up_hbm.at[0], up, w_sem.at[0])
    load_down = pltpu.make_async_copy(down_hbm.at[0], down, w_sem.at[1])
    load_up.start()
    load_down.start()

    ids = ids_ref[...]
    lanes = lax.broadcasted_iota(jnp.int32, (tok, 128), 1)
    picks = [(lanes == ids[:, k:k + 1]).astype(jnp.float32) for k in range(fanout)]
    named = functools.reduce(lambda a, b: a + b, picks).astype(bf)
    earlier = (
        lax.broadcasted_iota(jnp.int32, (tok, tok), 1)
        < lax.broadcasted_iota(jnp.int32, (tok, tok), 0)
    ).astype(jnp.float32).astype(bf)
    before = dot(earlier, named)
    slots = lax.broadcasted_iota(jnp.int32, (tok, n_ep * rows), 1).astype(jnp.float32)
    zero = jnp.zeros(slots.shape, jnp.float32)
    first, second, first_w, second_w = zero, zero, zero, zero
    for k in range(fanout):
        place = jnp.sum(picks[k] * before, axis=1, keepdims=True)
        target = ids[:, k:k + 1].astype(jnp.float32) * float(rows) + place
        weight = gate_ref[:, k:k + 1].astype(jnp.float32)
        hit, hit2 = slots == target, slots == target + float(cap)
        first = first + jnp.where(hit, 1.0, 0.0)
        first_w = first_w + jnp.where(hit, weight, 0.0)
        second = second + jnp.where(hit2, 1.0, 0.0)
        second_w = second_w + jnp.where(hit2, weight, 0.0)
    spread = jnp.concatenate([first, second_w], axis=0).astype(bf)
    route[...] = jnp.concatenate([first_w, second], axis=0).astype(bf)

    def sent_columns(h):
        cols = pl.ds(pl.multiple_of(h * half, 128), half)
        source = jnp.concatenate([x_ref[:, cols], g_ref[:, cols]], axis=0)
        return dot(spread, source, TN).astype(bf).reshape(n_ep, rows, half)

    disp[...] = sent_columns(c)
    pl.semaphore_wait(barrier, n_ep - 1 + n_dp - 1 + 1)

    def z_copy(dst, src):
        return pltpu.make_async_remote_copy(
            src_ref=disp.at[dst], dst_ref=recv.at[d, c, src],
            send_sem=z_send.at[dst], recv_sem=z_recv.at[src],
            device_id={"ep": dst}, device_id_type=MESH)

    def z_arrival(src):
        return pltpu.make_async_remote_copy(
            src_ref=disp.at[src], dst_ref=recv.at[d, c, src],
            send_sem=z_send.at[src], recv_sem=z_recv.at[src],
            device_id={"ep": src}, device_id_type=MESH)

    def x_copy(to, src):
        return pltpu.make_async_remote_copy(
            src_ref=recv.at[d, c, src], dst_ref=recv.at[d, c, src],
            send_sem=x_send.at[to, src], recv_sem=x_recv.at[d, src],
            device_id={"dp": to}, device_id_type=MESH)

    def x_arrival(frm, src):
        return pltpu.make_async_remote_copy(
            src_ref=recv.at[frm, c, src], dst_ref=recv.at[frm, c, src],
            send_sem=x_send.at[frm, src], recv_sem=x_recv.at[frm, src],
            device_id={"dp": frm}, device_id_type=MESH)

    def s_copy(group, src):
        return pltpu.make_async_remote_copy(
            src_ref=recv.at[group, c, src], dst_ref=recv.at[group, c, src],
            send_sem=s_send.at[group, src], recv_sem=s_recv.at[group, src],
            device_id={"tp": sib}, device_id_type=MESH)

    def s_arrival(group, src):
        return pltpu.make_async_remote_copy(
            src_ref=recv.at[group, sib, src], dst_ref=recv.at[group, sib, src],
            send_sem=s_send.at[group, src], recv_sem=s_recv.at[group, src],
            device_id={"tp": sib}, device_id_type=MESH)

    def p_copy(src):
        return pltpu.make_async_remote_copy(
            src_ref=part.at[src], dst_ref=got.at[src],
            send_sem=p_send.at[src], recv_sem=p_recv.at[src],
            device_id={"tp": sib}, device_id_type=MESH)

    def r_copy(src):
        return pltpu.make_async_remote_copy(
            src_ref=ret.at[src], dst_ref=back.at[z],
            send_sem=r_send.at[src], recv_sem=r_recv.at[z],
            device_id={"ep": src}, device_id_type=MESH)

    def r_arrival(exp):
        return pltpu.make_async_remote_copy(
            src_ref=ret.at[exp], dst_ref=back.at[exp],
            send_sem=r_send.at[exp], recv_sem=r_recv.at[exp],
            device_id={"ep": exp}, device_id_type=MESH)

    each((2, 3, 1), lambda i: z_copy(peer(i), z).start())

    other[...] = sent_columns(sib)
    recv[d, c, z] = disp[z]
    recv[d, sib, z] = other[z]
    for j in range(1, n_dp):
        x_copy(lax.rem(d + j, n_dp), z).start()
    load_up.wait()
    load_down.wait()

    def expert(group, src):
        left, right = recv[group, 0, src], recv[group, 1, src]
        left, right = left.astype(jnp.float32), right.astype(jnp.float32)
        r0, r1 = left[:cap].astype(bf), right[:cap].astype(bf)
        g0, g1 = left[cap:].astype(bf), right[cap:].astype(bf)
        preact = dot(r0, up[:half, :]) + dot(r1, up[half:, :])
        hidden_grad = dot(g0, down[:, :half], NT) + dot(g1, down[:, half:], NT)
        positive = jnp.maximum(preact, 0.0)
        hidden = positive * positive
        preact_grad = 2.0 * hidden_grad * positive
        nought = jnp.zeros_like(hidden)
        b_up[group, src] = jnp.concatenate([preact_grad, nought], axis=0).astype(bf)
        b_dn[group, src] = jnp.concatenate([nought, hidden], axis=0).astype(bf)
        return hidden.astype(bf), preact_grad.astype(bf)

    def columns_of(hidden, preact_grad, h):
        cols = pl.ds(pl.multiple_of(h * half, 128), half)
        return jnp.concatenate(
            [dot(hidden, down[:, cols]), dot(preact_grad, up[cols, :], NT)], axis=0)

    def first_pass(src):
        hidden, preact_grad = expert(d, src)
        part[src] = columns_of(hidden, preact_grad, sib).astype(bf)
        p_copy(src).start()
        mine[src] = columns_of(hidden, preact_grad, c)

    def finish(src):
        p_copy(src).wait_recv()
        return (mine[src] + got[src].astype(jnp.float32)).astype(bf)

    first_pass(z)

    def block(i):
        src, last = peer(i), peer(i - 1)
        z_arrival(src).wait_recv()
        s_copy(d, src).start()
        for j in range(1, n_dp):
            x_copy(lax.rem(d + j, n_dp), src).start()
        if isinstance(i, int):
            if i == 1:
                back[z] = finish(z)
            else:
                ret[last] = finish(last)
                r_copy(last).start()
        else:
            ret[last] = finish(last)

            @pl.when(i == 1)
            def _():
                back[z] = ret[z]

            @pl.when(i > 1)
            def _():
                r_copy(last).start()
        s_arrival(d, src).wait_recv()
        first_pass(src)

    each((1, 2, 3), block)
    end = peer(n_ep - 1)
    ret[end] = finish(end)
    r_copy(end).start()

    def pass_on(t, _):
        frm, src = lax.rem(d + 1 + t // n_ep, n_dp), lax.rem(z + t, n_ep)
        x_arrival(frm, src).wait_recv()
        s_copy(frm, src).start()
        return 0

    lax.fori_loop(0, (n_dp - 1) * n_ep, pass_on, 0)

    def replica(t, _):
        frm, src = lax.rem(d + 1 + t // n_ep, n_dp), lax.rem(z + t, n_ep)
        s_arrival(frm, src).wait_recv()
        expert(frm, src)
        return 0

    lax.fori_loop(0, (n_dp - 1) * n_ep, replica, 0)

    share = width // n_dp
    at = d * share

    def gradients(group, _):
        if share == half:
            held = recv[group, d]
        else:
            held = recv[group, at // half, :, :, pl.ds(
                pl.multiple_of(lax.rem(at, half), 128), share)]
        held = held.reshape(n_ep * rows, share)
        inner = b_up.shape[-1]
        gu[group] = dot(held, b_up[group].reshape(n_ep * rows, inner), TN).astype(bf)
        gd[group] = dot(b_dn[group].reshape(n_ep * rows, inner), held, TN).astype(bf)
        return 0

    lax.fori_loop(0, n_dp, gradients, 0)
    store_up = pltpu.make_async_copy(gu, gu_ref, o_sem.at[0])
    store_down = pltpu.make_async_copy(gd, gd_ref, o_sem.at[1])
    store_up.start()
    store_down.start()

    each((1, 2, 3), lambda i: r_arrival(peer(i)).wait_recv())
    total = dot(route[...], back[...].reshape(n_ep * rows, half))
    out_ref[...] = total[:tok].astype(bf)
    in_ref[...] = total[tok:].astype(bf)

    def drain(i):
        z_copy(peer(i), z).wait_send()
        s_copy(d, peer(i)).wait_send()
        r_copy(peer(i)).wait_send()

    each((1, 2, 3), drain)

    def drain_all(t, _):
        p_copy(t).wait_send()
        for j in range(1, n_dp):
            x_copy(lax.rem(d + j, n_dp), t).wait_send()
            s_copy(lax.rem(d + j, n_dp), t).wait_send()
        return 0

    lax.fori_loop(0, n_ep, drain_all, 0)
    store_up.wait()
    store_down.wait()


def body(mesh, latent_in, out_grad, expert_ids, gate_weights, up_weight, down_weight):
    n_ep, n_dp = mesh.shape["ep"], mesh.shape["dp"]
    tok, width = latent_in.shape
    inner = up_weight.shape[2]
    assert up_weight.shape[0] == 1 and mesh.shape["tp"] == 2
    cap = 9 * tok * expert_ids.shape[1] // (8 * n_ep)
    cap = -(-cap // 8) * 8
    rows, half, share = 2 * cap, width // 2, width // n_dp
    bf, f32 = jnp.bfloat16, jnp.float32
    vmem, anyw = pl.BlockSpec(memory_space=pltpu.VMEM), pl.BlockSpec(memory_space=pl.ANY)
    dma = pltpu.SemaphoreType.DMA
    block = (n_ep, rows, half)
    out, lin, gu, gd = pl.pallas_call(
        functools.partial(kernel, n_ep, n_dp, cap),
        out_shape=(
            jax.ShapeDtypeStruct((tok, half), bf),
            jax.ShapeDtypeStruct((tok, half), bf),
            jax.ShapeDtypeStruct((n_dp, share, inner), bf),
            jax.ShapeDtypeStruct((n_dp, inner, share), bf),
        ),
        in_specs=[vmem, vmem, vmem, vmem, anyw, anyw],
        out_specs=(vmem, vmem, anyw, anyw),
        scratch_shapes=[
            pltpu.VMEM((width, inner), bf),
            pltpu.VMEM((inner, width), bf),
            pltpu.VMEM(block, bf),
            pltpu.VMEM(block, bf),
            pltpu.VMEM((n_dp, 2) + block, bf),
            pltpu.VMEM((n_dp, n_ep, rows, inner), bf),
            pltpu.VMEM((n_dp, n_ep, rows, inner), bf),
            pltpu.VMEM(block, bf),
            pltpu.VMEM(block, bf),
            pltpu.VMEM(block, f32),
            pltpu.VMEM(block, bf),
            pltpu.VMEM(block, bf),
            pltpu.VMEM((n_dp, share, inner), bf),
            pltpu.VMEM((n_dp, inner, share), bf),
            pltpu.VMEM((2 * tok, n_ep * rows), bf),
            dma((2,)), dma((n_ep,)), dma((n_ep,)), dma((n_dp, n_ep)), dma((n_dp, n_ep)),
            dma((n_dp, n_ep)), dma((n_dp, n_ep)), dma((n_ep,)), dma((n_ep,)),
            dma((n_ep,)), dma((n_ep,)), dma((2,)),
        ],
        compiler_params=pltpu.CompilerParams(
            collective_id=0, has_side_effects=True, vmem_limit_bytes=48 * 1024 * 1024),
        name="routed_experts",
    )(latent_in, out_grad, expert_ids, gate_weights, up_weight, down_weight)
    grad_up = functools.reduce(lambda a, b: a + b, [gu[i].astype(f32) for i in range(n_dp)])
    grad_down = functools.reduce(lambda a, b: a + b, [gd[i].astype(f32) for i in range(n_dp)])
    return out, lin, grad_up[None], grad_down[None]


def solution(mesh):
    return jax.shard_map(
        functools.partial(body, mesh),
        mesh=mesh,
        in_specs=(
            P(("parts", "ep", "dp"), None),
            P(("parts", "ep", "dp"), None),
            P(("parts", "ep", "dp"), None),
            P(("parts", "ep", "dp"), None),
            P("ep", None, "tp"),
            P("ep", "tp", None),
        ),
        out_specs=(
            P(("parts", "ep", "dp"), "tp"),
            P(("parts", "ep", "dp"), "tp"),
            P(("parts", "ep"), "dp", "tp"),
            P(("parts", "ep"), "tp", "dp"),
        ),
        check_vma=False,
    )
```

time: 132 us -> 42.9 us (0.33)
  waiting for transfers between devices: 39.1 us -> 0 us
  Pallas kernels: 0 us -> 33.8 us
  starting transfers between devices: 26.8 us -> 0 us
  local copies, waits for them, and re-layouts: 25.5 us -> 6.56 us
  other arithmetic: 18.5 us -> 1.64 us
  between operations: 14 us -> 0.66 us
  matrix products: 7.14 us -> 0 us
    pallas_call x0 -> x1, Pallas kernels: none -> 33.8 us  [body(): pl.pallas_call(functools.partial(kernel, n_ep, n_dp, cap), out_shape=(jax...]
    all_to_all x4 -> x0, waiting for transfers between devices: 28 us -> none  [the longest x1 10.3 us: body(): lax.all_to_all(grads_in, 'ep', split_axis=0, concat_axis=1, tiled=True)]
    all_to_all x4 -> x0, starting transfers between devices: 26.5 us -> none  [the longest x1 7.65 us: body(): lax.all_to_all(output_part, 'ep', split_axis=1, concat_axis=0, tiled=True)]
    reduce_scatter x4 -> x0, waiting for transfers between devices: 11 us -> none  [the longest x1 11 us: body(): lax.psum_scatter(token_in.astype(jnp.bfloat16), 'tp', scatter_dimension=1...]
    unnamed x3 -> x0, other arithmetic: 9.05 us -> none
    dot_general x7 -> x0, matrix products: 7.14 us -> none  [the longest x1 1.73 us: body(): jnp.einsum('erf,erl->efl', hidden_state, recv_grads, preferred_element_ty...]
    gather x4 -> x0, local copies, waits for them, and re-layouts: 7.03 us -> none  [the longest x1 2.61 us: to_blocks(): gathered = jnp.concatenate([latent_cols, zero_row], axis=0)[source]]
    convert_element_type x4 -> x0, other arithmetic: 5.28 us -> none  [the longest x2 4.29 us: body(): grad_up, grad_down = (lax.psum_scatter(up_partial.astype(jnp.bfloat16), '...]
  transfers between devices with their start and end apart: 8 -> 0, of which waited for: 5 -> 0; matrix products, arithmetic and copies ran while one was open for 29% -> 0% of each run, Pallas kernels for 0% -> 0%
where the time goes in v1:
time: 42.9 us; the launch traced here: 42.6 us
  Pallas kernels  33.8 us (79%)
  local copies, waits for them, and re-layouts  6.56 us (15%)
  other arithmetic  1.64 us (4%)
  between operations  0.66 us (2%)
    pallas_call x1, Pallas kernels, body(): pl.pallas_call(functools.partial(kernel, n_ep, n_dp, cap), out_shape=(jax...  33.8 us
    unnamed x14, local copies, waits for them, and re-layouts  6.56 us
    add x1, other arithmetic, body(): a + b  1.64 us

profile of v1, /device:TPU:9, one launch (start us, length us, event | category | flops | bytes accessed | tf_op | source)
XLA Modules:
  0.0 42.6 jit_solution(15134920774447613073)
XLA Ops:
  0.6 0.0 copy-start.4
  0.6 0.8 %copy.11.gate_ref = bf16[128,2]{1,0:T(8,128)(2,1)S(1)} copy(bf16[128,2]{0,1:T(2,128)(2,1)} %param.9) | data formatting | bytes 1024 | tf_op args[3]
  1.4 0.0 copy-done.4
  1.4 0.1 copy.10.ids_ref
  1.5 0.0 copy-start
  1.6 1.2 %copy-done = bf16[1,1024,512]{2,1,0:T(8,128)(2,1)S(1)} copy-done((bf16[1,1024,512]{2,1,0:T(8,128)(2,1)S(1)}, bf16[1,1024,512]{2,1,0:T(8,128)(2,1)}, u32[]{:S(2)}) %copy-start) | copy-done | bytes 1048600
  2.8 0.0 copy-start.1
  2.8 1.2 %copy-done.1 = bf16[1,512,1024]{2,1,0:T(8,128)(2,1)S(1)} copy-done((bf16[1,512,1024]{2,1,0:T(8,128)(2,1)S(1)}, bf16[1,512,1024]{2,1,0:T(8,128)(2,1)}, u32[]{:S(2)}) %copy-start.1) | copy-done | bytes 1048600
  4.0 0.0 copy-start.2
  4.0 0.9 %copy-done.2 = bf16[128,1024]{1,0:T(8,128)(2,1)S(1)} copy-done((bf16[128,1024]{1,0:T(8,128)(2,1)S(1)}, bf16[128,1024]{1,0:T(8,128)(2,1)}, u32[]{:S(2)}) %copy-start.2) | copy-done | bytes 262168
  5.0 0.0 copy-start.3
  5.0 0.9 %copy-done.3 = bf16[128,1024]{1,0:T(8,128)(2,1)S(1)} copy-done((bf16[128,1024]{1,0:T(8,128)(2,1)S(1)}, bf16[128,1024]{1,0:T(8,128)(2,1)}, u32[]{:S(2)}) %copy-start.3) | copy-done | bytes 262168
  5.9 33.8 %routed_experts.1 = (bf16[128,512]{1,0:T(8,128)(2,1)S(1)}, bf16[128,512]{1,0:T(8,128)(2,1)S(1)}, bf16[2,512,512]{2,1,0:T(8,128)(2,1)S(1)}, bf16[2,512,512]{2,1,0:T(8,128)(2,1)S(1)}) custom-call(bf16[128,1024]{1,0:T(8,128)(2,1)S(1)} %copy-done.2, bf16[128,1024]{1,0:T(8,128)(2,1)S(1)} %copy-done.3, s32[128,2]{1,0:T(8,128)S(1)} %copy.10.ids_ref, ...), custom_call_target="tpu_custom_call" | custom-call | tf_op jit(solution)/shard_map/routed_experts/pallas_call | solution.py:295
  39.7 1.6 %convert_add_fusion = (f32[1,512,512]{2,1,0:T(8,128)}, f32[1,512,512]{2,1,0:T(8,128)}) fusion(bf16[2,512,512]{2,1,0:T(8,128)(2,1)S(1)} %get-tuple-element.11, bf16[2,512,512]{2,1,0:T(8,128)(2,1)S(1)} %get-tuple-element.10), kind=kLoop, calls=%fused_computation | loop fusion | flops 1572864 | bytes 4194304 | tf_op jit(solution)/shard_map/add | solution.py:330
  41.3 0.7 %copy.14 = bf16[128,512]{1,0:T(8,128)(2,1)} copy(bf16[128,512]{1,0:T(8,128)(2,1)S(1)} %get-tuple-element.18) | data formatting | bytes 262144
  42.0 0.7 %copy.15 = bf16[128,512]{1,0:T(8,128)(2,1)} copy(bf16[128,512]{1,0:T(8,128)(2,1)S(1)} %get-tuple-element.19) | data formatting | bytes 262144
Async XLA Ops:
  0.6 0.8 %copy-start.4 = (s32[128,2]{0,1:T(2,128)S(1)}, s32[128,2]{0,1:T(2,128)}, u32[]{:S(2)}) copy-start(s32[128,2]{0,1:T(2,128)} %param.8) | copy-start | bytes 3076
  1.5 1.2 %copy-start = (bf16[1,1024,512]{2,1,0:T(8,128)(2,1)S(1)}, bf16[1,1024,512]{2,1,0:T(8,128)(2,1)}, u32[]{:S(2)}) copy-start(bf16[1,1024,512]{2,1,0:T(8,128)(2,1)} %up_hbm.1) | copy-start | bytes 3145732
  2.8 1.2 %copy-start.1 = (bf16[1,512,1024]{2,1,0:T(8,128)(2,1)S(1)}, bf16[1,512,1024]{2,1,0:T(8,128)(2,1)}, u32[]{:S(2)}) copy-start(bf16[1,512,1024]{2,1,0:T(8,128)(2,1)} %down_hbm.1) | copy-start | bytes 3145732
  4.0 0.9 %copy-start.2 = (bf16[128,1024]{1,0:T(8,128)(2,1)S(1)}, bf16[128,1024]{1,0:T(8,128)(2,1)}, u32[]{:S(2)}) copy-start(bf16[128,1024]{1,0:T(8,128)(2,1)} %x_ref.1) | copy-start | bytes 786436
  5.0 0.9 %copy-start.3 = (bf16[128,1024]{1,0:T(8,128)(2,1)S(1)}, bf16[128,1024]{1,0:T(8,128)(2,1)}, u32[]{:S(2)}) copy-start(bf16[128,1024]{1,0:T(8,128)(2,1)} %g_ref.1) | copy-start | bytes 786436

commit v2 on v1

--- a/solution.py
+++ b/solution.py
@@ -18,9 +18,9 @@
 
 def kernel(
     n_ep, n_dp, cap,
-    x_ref, g_ref, ids_ref, gate_ref, up_hbm, down_hbm,
-    out_ref, in_ref, gu_ref, gd_ref,
-    up, down, disp, other, recv, b_up, b_dn, part, got, mine, ret, back, gu, gd, route,
+    x_hbm, g_hbm, ids_hbm, gate_hbm, up_hbm, down_hbm,
+    gu_ref, gd_ref, out_ref, in_ref,
+    x_ref, g_ref, ids_ref, gate_ref, up, down, disp, recv, b_up, b_dn, part, got, mine, ret, back, route, acc, gu, gd,
     w_sem, z_send, z_recv, s_send, s_recv, x_send, x_recv, p_send, p_recv, r_send, r_recv, o_sem,
 ):
     z, d, c = lax.axis_index("ep"), lax.axis_index("dp"), lax.axis_index("tp")
@@ -28,7 +28,7 @@
     rows = 2 * cap
     tok, width = x_ref.shape
     half = width // 2
-    fanout = ids_ref.shape[1]
+    fanout = ids_ref.shape[0]
     bf = jnp.bfloat16
 
     def peer(i):
@@ -43,6 +43,16 @@
         else:
             lax.fori_loop(1, n_ep, lambda i, _: (body(i), 0)[1], 0)
 
+    load_x = pltpu.make_async_copy(x_hbm, x_ref, w_sem.at[0])
+    load_g = pltpu.make_async_copy(g_hbm, g_ref, w_sem.at[1])
+    load_up = pltpu.make_async_copy(up_hbm.at[0], up, w_sem.at[2])
+    load_down = pltpu.make_async_copy(down_hbm.at[0], down, w_sem.at[3])
+    load_ids = pltpu.make_async_copy(ids_hbm, ids_ref, w_sem.at[4])
+    load_gate = pltpu.make_async_copy(gate_hbm, gate_ref, w_sem.at[5])
+    load_ids.start()
+    load_gate.start()
+    load_x.start()
+    load_g.start()
     barrier = pltpu.get_barrier_semaphore()
 
     def greet(i, _):
@@ -56,42 +66,46 @@
             barrier, inc=1, device_id={"dp": lax.rem(d + j, n_dp)}, device_id_type=MESH)
     pl.semaphore_signal(barrier, inc=1, device_id={"tp": sib}, device_id_type=MESH)
 
-    load_up = pltpu.make_async_copy(up_hbm.at[0], up, w_sem.at[0])
-    load_down = pltpu.make_async_copy(down_hbm.at[0], down, w_sem.at[1])
     load_up.start()
     load_down.start()
 
+    load_ids.wait()
+    load_gate.wait()
     ids = ids_ref[...]
-    lanes = lax.broadcasted_iota(jnp.int32, (tok, 128), 1)
-    picks = [(lanes == ids[:, k:k + 1]).astype(jnp.float32) for k in range(fanout)]
+    height = -(-n_ep // 16) * 16
+    numbers = lax.broadcasted_iota(jnp.int32, (height, tok), 0)
+    picks = [(numbers == ids[k:k + 1, :]).astype(jnp.float32) for k in range(fanout)]
     named = functools.reduce(lambda a, b: a + b, picks).astype(bf)
     earlier = (
-        lax.broadcasted_iota(jnp.int32, (tok, tok), 1)
-        < lax.broadcasted_iota(jnp.int32, (tok, tok), 0)
+        lax.broadcasted_iota(jnp.int32, (tok, tok), 0)
+        < lax.broadcasted_iota(jnp.int32, (tok, tok), 1)
     ).astype(jnp.float32).astype(bf)
-    before = dot(earlier, named)
-    slots = lax.broadcasted_iota(jnp.int32, (tok, n_ep * rows), 1).astype(jnp.float32)
-    zero = jnp.zeros(slots.shape, jnp.float32)
-    first, second, first_w, second_w = zero, zero, zero, zero
-    for k in range(fanout):
-        place = jnp.sum(picks[k] * before, axis=1, keepdims=True)
-        target = ids[:, k:k + 1].astype(jnp.float32) * float(rows) + place
-        weight = gate_ref[:, k:k + 1].astype(jnp.float32)
-        hit, hit2 = slots == target, slots == target + float(cap)
-        first = first + jnp.where(hit, 1.0, 0.0)
-        first_w = first_w + jnp.where(hit, weight, 0.0)
-        second = second + jnp.where(hit2, 1.0, 0.0)
-        second_w = second_w + jnp.where(hit2, weight, 0.0)
-    spread = jnp.concatenate([first, second_w], axis=0).astype(bf)
-    route[...] = jnp.concatenate([first_w, second], axis=0).astype(bf)
-
-    def sent_columns(h):
-        cols = pl.ds(pl.multiple_of(h * half, 128), half)
-        source = jnp.concatenate([x_ref[:, cols], g_ref[:, cols]], axis=0)
-        return dot(spread, source, TN).astype(bf).reshape(n_ep, rows, half)
-
-    disp[...] = sent_columns(c)
-    pl.semaphore_wait(barrier, n_ep - 1 + n_dp - 1 + 1)
+    before = dot(named, earlier)
+    gate = gate_ref[...].astype(jnp.float32)
+    targets = [
+        ids[k:k + 1, :].astype(jnp.float32) * float(rows)
+        + jnp.sum(picks[k] * before, axis=0, keepdims=True)
+        for k in range(fanout)]
+    row = lax.broadcasted_iota(jnp.int32, (rows, tok), 0)
+
+    def hits(exp, shift, weighted):
+        slots = (row + (exp * rows - shift)).astype(jnp.float32)
+        found = [
+            jnp.where(slots == targets[k], gate[k:k + 1, :] if weighted else 1.0, 0.0)
+            for k in range(fanout)]
+        return functools.reduce(lambda a, b: a + b, found)
+
+    def columns(h):
+        return pl.ds(pl.multiple_of(h * half, 128), half)
+
+    def build(exp, h):
+        spread = jnp.concatenate(
+            [hits(exp, 0, False), hits(exp, cap, True)], axis=1).astype(bf)
+        source = jnp.concatenate([x_ref[:, columns(h)], g_ref[:, columns(h)]], axis=0)
+        return dot(spread, source).astype(bf)
+
+    load_x.wait()
+    load_g.wait()
 
     def z_copy(dst, src):
         return pltpu.make_async_remote_copy(
@@ -147,13 +161,32 @@
             send_sem=r_send.at[exp], recv_sem=r_recv.at[exp],
             device_id={"ep": exp}, device_id_type=MESH)
 
-    each((2, 3, 1), lambda i: z_copy(peer(i), z).start())
-
-    other[...] = sent_columns(sib)
-    recv[d, c, z] = disp[z]
-    recv[d, sib, z] = other[z]
+    def send(i):
+        dst = peer(i)
+        disp[dst] = build(dst, c)
+        z_copy(dst, z).start()
+
+    if n_ep == 4:
+        disp[peer(2)] = build(peer(2), c)
+        pl.semaphore_wait(barrier, n_ep + n_dp - 1)
+        z_copy(peer(2), z).start()
+        send(1)
+        disp[peer(3)] = build(peer(3), c)
+    else:
+        pl.semaphore_wait(barrier, n_ep + n_dp - 1)
+        each((), send)
+
+    recv[d, c, z] = build(z, c)
+    recv[d, sib, z] = build(z, sib)
     for j in range(1, n_dp):
         x_copy(lax.rem(d + j, n_dp), z).start()
+
+    def weigh(exp, _):
+        route[exp] = jnp.concatenate(
+            [hits(exp, 0, True), hits(exp, cap, False)], axis=1).astype(bf)
+        return 0
+
+    lax.fori_loop(0, n_ep, weigh, 0)
     load_up.wait()
     load_down.wait()
 
@@ -188,6 +221,9 @@
         return (mine[src] + got[src].astype(jnp.float32)).astype(bf)
 
     first_pass(z)
+    if n_ep == 4:
+        z_copy(peer(2), z).wait_send()
+        z_copy(peer(3), z).start()
 
     def block(i):
         src, last = peer(i), peer(i - 1)
@@ -238,7 +274,7 @@
     share = width // n_dp
     at = d * share
 
-    def gradients(group, _):
+    def gradients(group):
         if share == half:
             held = recv[group, d]
         else:
@@ -246,23 +282,38 @@
                 pl.multiple_of(lax.rem(at, half), 128), share)]
         held = held.reshape(n_ep * rows, share)
         inner = b_up.shape[-1]
-        gu[group] = dot(held, b_up[group].reshape(n_ep * rows, inner), TN).astype(bf)
-        gd[group] = dot(b_dn[group].reshape(n_ep * rows, inner), held, TN).astype(bf)
-        return 0
-
-    lax.fori_loop(0, n_dp, gradients, 0)
+        grad_up = dot(held, b_up[group].reshape(n_ep * rows, inner), TN)
+        grad_down = dot(b_dn[group].reshape(n_ep * rows, inner), held, TN)
+        return grad_up.astype(bf).astype(jnp.float32), grad_down.astype(bf).astype(jnp.float32)
+
+    gu[...], gd[...] = gradients(0)
+
+    def add_group(group, _):
+        grad_up, grad_down = gradients(group)
+        gu[...] += grad_up
+        gd[...] += grad_down
+        return 0
+
+    lax.fori_loop(1, n_dp, add_group, 0)
     store_up = pltpu.make_async_copy(gu, gu_ref, o_sem.at[0])
     store_down = pltpu.make_async_copy(gd, gd_ref, o_sem.at[1])
     store_up.start()
     store_down.start()
 
-    each((1, 2, 3), lambda i: r_arrival(peer(i)).wait_recv())
-    total = dot(route[...], back[...].reshape(n_ep * rows, half))
-    out_ref[...] = total[:tok].astype(bf)
-    in_ref[...] = total[tok:].astype(bf)
+    acc[...] = dot(route[z], back[z], TN)
+
+    def collect(i):
+        exp = peer(i)
+        r_arrival(exp).wait_recv()
+        acc[...] += dot(route[exp], back[exp], TN)
+
+    each((1, 2, 3), collect)
+    out_ref[...] = acc[:tok].astype(bf)
+    in_ref[...] = acc[tok:].astype(bf)
 
     def drain(i):
-        z_copy(peer(i), z).wait_send()
+        if n_ep != 4 or i != 2:
+            z_copy(peer(i), z).wait_send()
         s_copy(d, peer(i)).wait_send()
         r_copy(peer(i)).wait_send()
 
@@ -276,8 +327,32 @@
         return 0
 
     lax.fori_loop(0, n_ep, drain_all, 0)
+
     store_up.wait()
     store_down.wait()
+
+
+def write_out(*refs):
+    n = (len(refs) - 2) // 3
+    sources, results, held = refs[:n], refs[n:2 * n], refs[2 * n:3 * n]
+    in_sem, out_sem = refs[3 * n:]
+    loads, stores = [], []
+    for i in range(n):
+        size = sources[i].shape[0]
+        step = 128 if size % 128 == 0 else size
+        for at in range(0, size, step):
+            part, j = pl.ds(at, step), len(loads)
+            loads.append(pltpu.make_async_copy(
+                sources[i].at[part], held[i].at[part], in_sem.at[j]))
+            stores.append(pltpu.make_async_copy(
+                held[i].at[part], results[i].at[part], out_sem.at[j]))
+    for load in loads:
+        load.start()
+    for load, store in zip(loads, stores):
+        load.wait()
+        store.start()
+    for store in stores:
+        store.wait()
 
 
 def body(mesh, latent_in, out_grad, expert_ids, gate_weights, up_weight, down_weight):
@@ -289,23 +364,28 @@
     cap = -(-cap // 8) * 8
     rows, half, share = 2 * cap, width // 2, width // n_dp
     bf, f32 = jnp.bfloat16, jnp.float32
-    vmem, anyw = pl.BlockSpec(memory_space=pltpu.VMEM), pl.BlockSpec(memory_space=pl.ANY)
+    vmem = pl.BlockSpec(memory_space=pltpu.VMEM)
+    hbm = pl.BlockSpec(memory_space=pltpu.HBM)
     dma = pltpu.SemaphoreType.DMA
     block = (n_ep, rows, half)
-    out, lin, gu, gd = pl.pallas_call(
+    results = (
+        jax.ShapeDtypeStruct((share, inner), f32),
+        jax.ShapeDtypeStruct((inner, share), f32),
+        jax.ShapeDtypeStruct((tok, half), bf),
+        jax.ShapeDtypeStruct((tok, half), bf),
+    )
+    held = pl.pallas_call(
         functools.partial(kernel, n_ep, n_dp, cap),
-        out_shape=(
-            jax.ShapeDtypeStruct((tok, half), bf),
-            jax.ShapeDtypeStruct((tok, half), bf),
-            jax.ShapeDtypeStruct((n_dp, share, inner), bf),
-            jax.ShapeDtypeStruct((n_dp, inner, share), bf),
-        ),
-        in_specs=[vmem, vmem, vmem, vmem, anyw, anyw],
-        out_specs=(vmem, vmem, anyw, anyw),
+        out_shape=results,
+        in_specs=[hbm] * 6,
+        out_specs=(hbm, hbm, vmem, vmem),
         scratch_shapes=[
+            pltpu.VMEM((tok, width), bf),
+            pltpu.VMEM((tok, width), bf),
+            pltpu.VMEM(expert_ids.shape[::-1], jnp.int32),
+            pltpu.VMEM(gate_weights.shape[::-1], bf),
             pltpu.VMEM((width, inner), bf),
             pltpu.VMEM((inner, width), bf),
-            pltpu.VMEM(block, bf),
             pltpu.VMEM(block, bf),
             pltpu.VMEM((n_dp, 2) + block, bf),
             pltpu.VMEM((n_dp, n_ep, rows, inner), bf),
@@ -315,19 +395,28 @@
             pltpu.VMEM(block, f32),
             pltpu.VMEM(block, bf),
             pltpu.VMEM(block, bf),
-            pltpu.VMEM((n_dp, share, inner), bf),
-            pltpu.VMEM((n_dp, inner, share), bf),
-            pltpu.VMEM((2 * tok, n_ep * rows), bf),
-            dma((2,)), dma((n_ep,)), dma((n_ep,)), dma((n_dp, n_ep)), dma((n_dp, n_ep)),
+            pltpu.VMEM((n_ep, rows, 2 * tok), bf),
+            pltpu.VMEM((2 * tok, half), f32),
+            pltpu.VMEM((share, inner), f32),
+            pltpu.VMEM((inner, share), f32),
+            dma((6,)), dma((n_ep,)), dma((n_ep,)), dma((n_dp, n_ep)), dma((n_dp, n_ep)),
             dma((n_dp, n_ep)), dma((n_dp, n_ep)), dma((n_ep,)), dma((n_ep,)),
             dma((n_ep,)), dma((n_ep,)), dma((2,)),
         ],
         compiler_params=pltpu.CompilerParams(
-            collective_id=0, has_side_effects=True, vmem_limit_bytes=48 * 1024 * 1024),
+            collective_id=0, has_side_effects=True, vmem_limit_bytes=58 * 1024 * 1024),
         name="routed_experts",
-    )(latent_in, out_grad, expert_ids, gate_weights, up_weight, down_weight)
-    grad_up = functools.reduce(lambda a, b: a + b, [gu[i].astype(f32) for i in range(n_dp)])
-    grad_down = functools.reduce(lambda a, b: a + b, [gd[i].astype(f32) for i in range(n_dp)])
+    )(latent_in, out_grad, expert_ids.T, gate_weights.T, up_weight, down_weight)
+    count = sum(-(-r.shape[0] // 128) for r in results)
+    grad_up, grad_down, out, lin = pl.pallas_call(
+        write_out,
+        out_shape=results,
+        in_specs=[hbm] * 4,
+        out_specs=(hbm,) * 4,
+        scratch_shapes=[pltpu.VMEM(r.shape, r.dtype) for r in results] + [dma((count,))] * 2,
+        compiler_params=pltpu.CompilerParams(vmem_limit_bytes=58 * 1024 * 1024),
+        name="write_out",
+    )(*held)
     return out, lin, grad_up[None], grad_down[None]
 
 

time: 42.9 us -> 35.4 us (0.83)
  local copies, waits for them, and re-layouts: 6.56 us -> 0 us
  other arithmetic: 1.64 us -> 0 us
  Pallas kernels: 33.8 us -> 34.6 us
    unnamed x14 -> x0, local copies, waits for them, and re-layouts: 6.56 us -> none
    add x1 -> x0, other arithmetic: 1.64 us -> none  [body(): a + b]
    pallas_call x1 -> x2, Pallas kernels: 33.8 us -> 34.6 us  [the longest x1 32.1 us: body(): pl.pallas_call(functools.partial(kernel, n_ep, n_dp, cap), out_shape=resu...]
where the time goes in v2:
time: 35.4 us; the launch traced here: 35.2 us
  Pallas kernels  34.6 us (98%)
  between operations  0.64 us (2%)
    pallas_call x1, Pallas kernels, body(): pl.pallas_call(functools.partial(kernel, n_ep, n_dp, cap), out_shape=resu...  32.1 us
    pallas_call x1, Pallas kernels, body(): pl.pallas_call(write_out, out_shape=results, in_specs=[hbm] * 4, out_spec...  2.51 us

profile of v2, /device:TPU:9, one launch (start us, length us, event | category | flops | bytes accessed | tf_op | source)
XLA Modules:
  0.0 35.2 jit_solution(10973713219498729391)
XLA Ops:
  0.6 32.1 %routed_experts.1 = (f32[512,512]{1,0:T(8,128)}, f32[512,512]{1,0:T(8,128)}, bf16[128,512]{1,0:T(8,128)(2,1)}, bf16[128,512]{1,0:T(8,128)(2,1)}) custom-call(bf16[128,1024]{1,0:T(8,128)(2,1)} %x_hbm.1, bf16[128,1024]{1,0:T(8,128)(2,1)} %g_hbm.1, s32[2,128]{1,0:T(2,128)} %bitcast.4, bf16[2,128]{1,0:T(2,128)(2,1)} %bitcast.5, bf16[1,1024,512]{2,1,0:T(8,128)(2,1)} %up_hbm.1, ...), custom_call_target="tpu_custom_call" | custom-call | tf_op jit(solution)/shard_map/routed_experts/pallas_call | solution.py:377
  32.7 2.5 %write_out.1 = (f32[512,512]{1,0:T(8,128)}, f32[512,512]{1,0:T(8,128)}, bf16[128,512]{1,0:T(8,128)(2,1)}, bf16[128,512]{1,0:T(8,128)(2,1)}) custom-call(f32[512,512]{1,0:T(8,128)} %get-tuple-element.12.refs_0_, f32[512,512]{1,0:T(8,128)} %get-tuple-element.13.refs_1_, bf16[128,512]{1,0:T(8,128)(2,1)} %get-tuple-element.14.refs_2_, ...), custom_call_target="tpu_custom_call" | custom-call | tf_op jit(solution)/shard_map/write_out/pallas_call | solution.py:411

commit v3 on v2

--- a/solution.py
+++ b/solution.py
@@ -220,33 +220,33 @@
         p_copy(src).wait_recv()
         return (mine[src] + got[src].astype(jnp.float32)).astype(bf)
 
-    first_pass(z)
     if n_ep == 4:
         z_copy(peer(2), z).wait_send()
         z_copy(peer(3), z).start()
+    first_pass(z)
 
     def block(i):
         src, last = peer(i), peer(i - 1)
+        if isinstance(i, int):
+            if i > 1:
+                ret[last] = finish(last)
+                r_copy(last).start()
+        else:
+            ret[last] = finish(last)
+
+            @pl.when(i == 1)
+            def _():
+                back[z] = ret[z]
+
+            @pl.when(i > 1)
+            def _():
+                r_copy(last).start()
         z_arrival(src).wait_recv()
         s_copy(d, src).start()
         for j in range(1, n_dp):
             x_copy(lax.rem(d + j, n_dp), src).start()
-        if isinstance(i, int):
-            if i == 1:
-                back[z] = finish(z)
-            else:
-                ret[last] = finish(last)
-                r_copy(last).start()
-        else:
-            ret[last] = finish(last)
-
-            @pl.when(i == 1)
-            def _():
-                back[z] = ret[z]
-
-            @pl.when(i > 1)
-            def _():
-                r_copy(last).start()
+        if isinstance(i, int) and i == 1:
+            back[z] = finish(z)
         s_arrival(d, src).wait_recv()
         first_pass(src)
 

time: 35.4 us -> 35.3 us (level)
  no operation moved by 1% of the time
where the time goes in v3:
time: 35.3 us; the launch traced here: 35.1 us
  Pallas kernels  34.5 us (98%)
  between operations  0.64 us (2%)
    pallas_call x1, Pallas kernels, body(): pl.pallas_call(functools.partial(kernel, n_ep, n_dp, cap), out_shape=resu...  32 us
    pallas_call x1, Pallas kernels, body(): pl.pallas_call(write_out, out_shape=results, in_specs=[hbm] * 4, out_spec...  2.51 us

profile of v3, /device:TPU:9, one launch (start us, length us, event | category | flops | bytes accessed | tf_op | source)
XLA Modules:
  0.0 35.1 jit_solution(11162140125644684079)
XLA Ops:
  0.6 32.0 %routed_experts.1 = (f32[512,512]{1,0:T(8,128)}, f32[512,512]{1,0:T(8,128)}, bf16[128,512]{1,0:T(8,128)(2,1)}, bf16[128,512]{1,0:T(8,128)(2,1)}) custom-call(bf16[128,1024]{1,0:T(8,128)(2,1)} %x_hbm.1, bf16[128,1024]{1,0:T(8,128)(2,1)} %g_hbm.1, s32[2,128]{1,0:T(2,128)} %bitcast.4, bf16[2,128]{1,0:T(2,128)(2,1)} %bitcast.5, bf16[1,1024,512]{2,1,0:T(8,128)(2,1)} %up_hbm.1, ...), custom_call_target="tpu_custom_call" | custom-call | tf_op jit(solution)/shard_map/routed_experts/pallas_call | solution.py:377
  32.6 2.5 %write_out.1 = (f32[512,512]{1,0:T(8,128)}, f32[512,512]{1,0:T(8,128)}, bf16[128,512]{1,0:T(8,128)(2,1)}, bf16[128,512]{1,0:T(8,128)(2,1)}) custom-call(f32[512,512]{1,0:T(8,128)} %get-tuple-element.12.refs_0_, f32[512,512]{1,0:T(8,128)} %get-tuple-element.13.refs_1_, bf16[128,512]{1,0:T(8,128)(2,1)} %get-tuple-element.14.refs_2_, ...), custom_call_target="tpu_custom_call" | custom-call | tf_op jit(solution)/shard_map/write_out/pallas_call | solution.py:411

commit v4 on v3

--- a/solution.py
+++ b/solution.py
@@ -66,8 +66,6 @@
             barrier, inc=1, device_id={"dp": lax.rem(d + j, n_dp)}, device_id_type=MESH)
     pl.semaphore_signal(barrier, inc=1, device_id={"tp": sib}, device_id_type=MESH)
 
-    load_up.start()
-    load_down.start()
 
     load_ids.wait()
     load_gate.wait()
@@ -106,6 +104,8 @@
 
     load_x.wait()
     load_g.wait()
+    load_up.start()
+    load_down.start()
 
     def z_copy(dst, src):
         return pltpu.make_async_remote_copy(
@@ -339,7 +339,7 @@
     loads, stores = [], []
     for i in range(n):
         size = sources[i].shape[0]
-        step = 128 if size % 128 == 0 else size
+        step = 256 if size % 256 == 0 else size
         for at in range(0, size, step):
             part, j = pl.ds(at, step), len(loads)
             loads.append(pltpu.make_async_copy(
@@ -407,7 +407,7 @@
             collective_id=0, has_side_effects=True, vmem_limit_bytes=58 * 1024 * 1024),
         name="routed_experts",
     )(latent_in, out_grad, expert_ids.T, gate_weights.T, up_weight, down_weight)
-    count = sum(-(-r.shape[0] // 128) for r in results)
+    count = sum(-(-r.shape[0] // 256) for r in results)
     grad_up, grad_down, out, lin = pl.pallas_call(
         write_out,
         out_shape=results,

time: 35.3 us -> 35.3 us (level)
  no operation moved by 1% of the time
where the time goes in v4:
time: 35.3 us; the launch traced here: 35.2 us
  Pallas kernels  34.5 us (98%)
  between operations  0.64 us (2%)
    pallas_call x1, Pallas kernels, body(): pl.pallas_call(functools.partial(kernel, n_ep, n_dp, cap), out_shape=resu...  32 us
    pallas_call x1, Pallas kernels, body(): pl.pallas_call(write_out, out_shape=results, in_specs=[hbm] * 4, out_spec...  2.54 us

profile of v4, /device:TPU:9, one launch (start us, length us, event | category | flops | bytes accessed | tf_op | source)
XLA Modules:
  0.0 35.2 jit_solution(6095853094960164756)
XLA Ops:
  0.6 32.0 %routed_experts.1 = (f32[512,512]{1,0:T(8,128)}, f32[512,512]{1,0:T(8,128)}, bf16[128,512]{1,0:T(8,128)(2,1)}, bf16[128,512]{1,0:T(8,128)(2,1)}) custom-call(bf16[128,1024]{1,0:T(8,128)(2,1)} %x_hbm.1, bf16[128,1024]{1,0:T(8,128)(2,1)} %g_hbm.1, s32[2,128]{1,0:T(2,128)} %bitcast.4, bf16[2,128]{1,0:T(2,128)(2,1)} %bitcast.5, bf16[1,1024,512]{2,1,0:T(8,128)(2,1)} %up_hbm.1, ...), custom_call_target="tpu_custom_call" | custom-call | tf_op jit(solution)/shard_map/routed_experts/pallas_call | solution.py:377
  32.6 2.5 %write_out.1 = (f32[512,512]{1,0:T(8,128)}, f32[512,512]{1,0:T(8,128)}, bf16[128,512]{1,0:T(8,128)(2,1)}, bf16[128,512]{1,0:T(8,128)(2,1)}) custom-call(f32[512,512]{1,0:T(8,128)} %get-tuple-element.12.refs_0_, f32[512,512]{1,0:T(8,128)} %get-tuple-element.13.refs_1_, bf16[128,512]{1,0:T(8,128)(2,1)} %get-tuple-element.14.refs_2_, ...), custom_call_target="tpu_custom_call" | custom-call | tf_op jit(solution)/shard_map/write_out/pallas_call | solution.py:411
